TPU v7x, 32 devices: a whole 2x2x4 slice. The times are simulated.
32 devices in a mesh: group: 2 (over x), replica: 16 (over z, y, core).
Axes of the slice: x: 2, y: 2, z: 4, core: 2. Of those that a mesh axis runs over, the one named last changes fastest.
Arguments:
- hidden: bfloat16 [256, 8192], P(('group', 'replica')), parts along dimension 0, may hold values from -6 to 6
- input_norm_gain: float32 [8192], replicated, may hold values from 0.1 to 1.9
- row_adapter_index: int32 [256, 1], P(('group', 'replica')), parts along dimension 0, may hold values from 0 to 15; in each aligned block of 128 rows (0 to 127, 128 to 255, ...) at most 16 rows name the same one
- adapter_slot_table: int32 [16], replicated, may hold values from 0 to 15, each once
- cache_length: int32 [256], P(('group', 'replica')), parts along dimension 0, may hold values from 1 to 96, as said below
- rotated_key_cache: bfloat16 [256, 96, 1024], P(('group', 'replica')), parts along dimension 0, may hold values from -480 to 480
- cached_value_table: bfloat16 [256, 96, 1024], P(('group', 'replica')), parts along dimension 0, may hold values from -6 to 6
- query_weight: bfloat16 [8192, 8192], P(None, 'replica'), may hold values from -0.0625 to 0.0625
- key_value_weight: bfloat16 [2, 1024, 8192], P(None, 'replica'), may hold values from -0.0625 to 0.0625
- output_weight: bfloat16 [8192, 8192], P(None, 'replica'), may hold values from -0.25 to 0.25
- adapter_down_weight: bfloat16 [16, 4, 64, 8192], P('replica'), may hold values from -0.0625 to 0.0625
- query_up_weight: bfloat16 [16, 64, 8192], P('replica'), may hold values from -0.75 to 0.75
- key_value_up_weight: bfloat16 [16, 2, 64, 1024], P('replica'), may hold values from -0.75 to 0.75
- output_up_weight: bfloat16 [16, 64, 8192], P('replica'), may hold values from -0.75 to 0.75
Outputs:
- attn_out: bfloat16 [256, 8192], P(('group', 'replica')), parts along dimension 0
There are 2 independent parts, one for each index of `group`. A program takes and returns all parts, laid end to end along the dimension named above; an argument that names none is the same for every part. Nothing has to cross between parts.
Inputs may be any that keep to these rules, and one draw needn't show every extreme that they name: `row_adapter_index`: no adapter is named by more than 16 of the 128 rows of a group. `adapter_slot_table`: each slot once. `cache_length`: among the rows of each replica one has length 96.
All inputs are finite; a program needn't handle non-finite values.
Results may differ from a plain program's by a relative error of at most 0.0075.
The roundings to bfloat16 on the way count: a program that leaves them out, or rounds other values in their place, can miss the bound.
Values may be sent and summed in bfloat16 or wider, within the bound.
A program may use at most 128 MiB of HBM per device.

v0:
```python
import math

import jax
import jax.numpy as jnp
from jax import lax
from jax.sharding import PartitionSpec as P

HEADS = 64
KV_HEADS = 8
HD = 128
LENGTH = 96


adapter_scale = 0.5


def rms_norm(hidden, input_norm_gain):
    values = hidden.astype(jnp.float32)
    scaled = values * lax.rsqrt(jnp.mean(values * values, axis=-1, keepdims=True) + 1e-06)
    return (scaled * input_norm_gain).astype(jnp.bfloat16)


def rotate(values, position):
    half_width = HD // 2
    inv_freq = 1000000.0 ** (-(jnp.arange(half_width, dtype=jnp.float32) * 2.0 / HD))
    angles = position.astype(jnp.float32)[:, None, None] * inv_freq[None, None, :]
    cosine = jnp.concatenate([jnp.cos(angles), jnp.cos(angles)], axis=-1)
    sine_part = jnp.concatenate([jnp.sin(angles), jnp.sin(angles)], axis=-1)
    rotated = jnp.concatenate([-values[..., half_width:], values[..., :half_width]], axis=-1)
    return values * cosine + rotated * sine_part


def attend(queries, new_keys, new_values, cache_length, rotated_key_cache, cached_value_table):
    row_count = queries.shape[0]
    groups = HEADS // KV_HEADS
    scale_factor = 1.0 / math.sqrt(HD)
    heads_q = rotate(
        queries.astype(jnp.float32).reshape(row_count, HEADS, HD), cache_length
    ).astype(jnp.bfloat16)
    heads_k = rotate(
        new_keys.astype(jnp.float32).reshape(row_count, KV_HEADS, HD), cache_length
    ).astype(jnp.bfloat16)
    grouped_q = heads_q.reshape(row_count, KV_HEADS, groups, HD)
    cached_k = rotated_key_cache.reshape(row_count, LENGTH, KV_HEADS, HD)
    cached_v = cached_value_table.reshape(row_count, LENGTH, KV_HEADS, HD)
    scores = (
        jnp.einsum("rgjd,rtgd->rgjt", grouped_q, cached_k, preferred_element_type=jnp.float32)
        * scale_factor
    )
    own_score = (
        jnp.einsum("rgjd,rgd->rgj", grouped_q, heads_k, preferred_element_type=jnp.float32)
        * scale_factor
    )
    visible = (jnp.arange(LENGTH)[None, :] < cache_length[:, None])[:, None, None, :]
    masked = jnp.where(visible, scores, -1e30)
    largest = jnp.maximum(jnp.max(masked, axis=-1), own_score)
    weights = jnp.where(visible, jnp.exp(masked - largest[..., None]), 0.0)
    own_weight = jnp.exp(own_score - largest)
    denominator = jnp.sum(weights, axis=-1) + own_weight
    chances = (weights / denominator[..., None]).astype(jnp.bfloat16)
    own_chance = (own_weight / denominator).astype(jnp.bfloat16)
    mixed_values = jnp.einsum(
        "rgjt,rtgd->rgjd", chances, cached_v, preferred_element_type=jnp.float32
    )
    mixed_values = mixed_values + own_chance.astype(jnp.float32)[..., None] * new_values.astype(
        jnp.float32
    ).reshape(row_count, KV_HEADS, 1, HD)
    return mixed_values.reshape(row_count, HEADS * HD).astype(jnp.bfloat16)


def local(
    hidden,
    input_norm_gain,
    row_adapter_index,
    adapter_slot_table,
    cache_length,
    rotated_key_cache,
    cached_value_table,
    query_weight,
    key_value_weight,
    output_weight,
    adapter_down_weight,
    query_up_weight,
    key_value_up_weight,
    output_up_weight,
):
    devices = lax.axis_size("replica")
    myself = lax.axis_index("replica")
    local_rows = hidden.shape[0]
    capacity = 2 * local_rows
    adapters = adapter_slot_table.shape[0]
    normalized_input = rms_norm(hidden, input_norm_gain)
    picked = (row_adapter_index == jnp.arange(adapters)[None, :]).astype(jnp.int32)
    owner_devices = jnp.sum(picked * adapter_slot_table[None, :], axis=1)
    all_normed, all_owners = (
        lax.all_gather(normalized_input, "replica", axis=0, tiled=True),
        lax.all_gather(owner_devices, "replica", axis=0, tiled=True),
    )
    member = (all_owners[:, None] == jnp.arange(devices)[None, :]).astype(jnp.int32)
    running = jnp.cumsum(member, axis=0)
    position = all_owners * capacity + jnp.sum(running * member, axis=1) - 1
    my_slots = myself * capacity + jnp.arange(capacity)
    select = (position[None, :] == my_slots[:, None]).astype(jnp.bfloat16)
    my_rows = jnp.dot(select, all_normed, preferred_element_type=jnp.float32).astype(jnp.bfloat16)
    down_weight_maps = adapter_down_weight[0]
    factor_list = jnp.einsum(
        "cd,prd->cpr", my_rows, down_weight_maps[:3], preferred_element_type=jnp.float32
    ).astype(jnp.bfloat16)
    query_update = (
        adapter_scale
        * jnp.dot(factor_list[:, 0], query_up_weight[0], preferred_element_type=jnp.float32)
    ).astype(jnp.bfloat16)
    key_update = (
        adapter_scale
        * jnp.dot(factor_list[:, 1], key_value_up_weight[0, 0], preferred_element_type=jnp.float32)
    ).astype(jnp.bfloat16)
    value_update = (
        adapter_scale
        * jnp.dot(factor_list[:, 2], key_value_up_weight[0, 1], preferred_element_type=jnp.float32)
    ).astype(jnp.bfloat16)
    slot_q, slot_k, slot_v = (
        lax.all_to_all(query_update, "replica", split_axis=1, concat_axis=0, tiled=True),
        lax.all_to_all(key_update, "replica", split_axis=1, concat_axis=0, tiled=True),
        lax.all_to_all(value_update, "replica", split_axis=1, concat_axis=0, tiled=True),
    )
    contract = (((1,), (1,)), ((), ()))
    queries = jnp.dot(all_normed, query_weight, preferred_element_type=jnp.float32) + jnp.take(
        slot_q, position, axis=0
    ).astype(jnp.float32)
    key_new = lax.dot_general(
        all_normed, key_value_weight[0], contract, preferred_element_type=jnp.float32
    ) + jnp.take(slot_k, position, axis=0).astype(jnp.float32)
    value_new = lax.dot_general(
        all_normed, key_value_weight[1], contract, preferred_element_type=jnp.float32
    ) + jnp.take(slot_v, position, axis=0).astype(jnp.float32)
    q_rows, k_rows, v_rows = (
        lax.all_to_all(
            queries.astype(jnp.bfloat16), "replica", split_axis=0, concat_axis=1, tiled=True
        ),
        lax.all_to_all(
            key_new.astype(jnp.bfloat16), "replica", split_axis=0, concat_axis=1, tiled=True
        ),
        lax.all_to_all(
            value_new.astype(jnp.bfloat16), "replica", split_axis=0, concat_axis=1, tiled=True
        ),
    )
    attention_result = attend(
        q_rows, k_rows, v_rows, cache_length, rotated_key_cache, cached_value_table
    )
    attended_all = lax.all_gather(attention_result, "replica", axis=0, tiled=True)
    my_attended = jnp.dot(select, attended_all, preferred_element_type=jnp.float32).astype(
        jnp.bfloat16
    )
    output_factor = lax.dot_general(
        my_attended, down_weight_maps[3], contract, preferred_element_type=jnp.float32
    ).astype(jnp.bfloat16)
    output_update = adapter_scale * jnp.dot(
        output_factor, output_up_weight[0], preferred_element_type=jnp.float32
    )
    delta_cols = lax.all_to_all(
        output_update.astype(jnp.bfloat16), "replica", split_axis=1, concat_axis=0, tiled=True
    ).astype(output_update.dtype)
    partial_cols = jnp.dot(
        attended_all, output_weight, preferred_element_type=jnp.float32
    ) + jnp.take(delta_cols, position, axis=0)
    return lax.all_to_all(
        partial_cols.astype(jnp.bfloat16), "replica", split_axis=0, concat_axis=1, tiled=True
    )


def solution(mesh):
    in_specs = (
        P(("group", "replica"), None),
        P(),
        P(("group", "replica"), None),
        P(),
        P(("group", "replica")),
        P(("group", "replica"), None, None),
        P(("group", "replica"), None, None),
        P(None, "replica"),
        P(None, "replica", None),
        P(None, "replica"),
        P("replica", None, None, None),
        P("replica", None, None),
        P("replica", None, None, None),
        P("replica", None, None),
    )
    out_specs = P(("group", "replica"), None)
    return jax.shard_map(local, mesh=mesh, in_specs=in_specs, out_specs=out_specs, check_vma=False)
```

profile of v0, /device:TPU:0, one launch (start us, length us, event | category | flops | bytes accessed | tf_op | source)
XLA Modules:
  0.0 215.7 jit_solution(2690721692790540638)
XLA Ops:
  6.5 1.2 fusion.48
  7.8 1.7 fusion.50
  9.4 0.7 convert_element_type.142
  10.1 1.3 dynamic-slice
  12.0 0.9 select_reduce_fusion.1
  12.9 0.2 dynamic-update-slice
  13.1 13.7 %all-reduce = s32[128]{0:T(128)S(1)} all-reduce(s32[128]{0:T(128)S(1)} %dynamic-update-slice), channel_id=1, replica_groups=mesh['group'=2,'replica'=16] {'replica'}, use_global_device_ids=true, to_apply=%add | all-reduce | flops 128 | bytes 1024
  26.9 0.2 reduce_window_sum.11
  27.1 0.2 select_reduce_fusion
  27.3 0.7 iota_compare_fusion.2
  28.1 0.1 multiply_cosine_fusion
  28.2 25.5 %all-gather.3.cloned.1.call-done = bf16[128,8192]{1,0:T(8,128)(2,1)} async-done(((bf16[8,8192]{1,0:T(8,128)(2,1)}), bf16[128,8192]{1,0:T(8,128)(2,1)}) %all-gather.3.cloned.1.call-update) | async-done | bytes 2097168 | tf_op jit(solution)/shard_map/all_gather | solution.py:96
  53.7 4.0 %fusion.36 = bf16[16,3,64]{2,0,1:T(8,128)(2,1)S(1)} fusion(bf16[1,4,64,8192]{3,2,1,0:T(8,128)(2,1)} %param.26, bf16[128,8192]{1,0:T(8,128)(2,1)} %all-gather.3.cloned.1.call-done, s32[128]{0:T(128)S(1)} %broadcast_add_fusion, s32[16]{0:T(128)S(1)} %iota_add_fusion), kind=kOutput, calls=%fused_computation.40 | convolution fusion | flops 84022272 | bytes 5249600 | tf_op jit(solution)/shard_map/cd,prd->cpr/dot_general | solution.py:106
  57.7 0.2 fusion.33
  57.9 0.1 all_to_all.108
  58.0 0.7 reshape.254
  58.8 3.5 %all-to-all-start.4 = ((bf16[16,2,512]{2,1,0:T(2,128)(2,1)}), bf16[16,2,512]{2,1,0:T(2,128)(2,1)S(1)}, u32[]{:S(2)}, u32[]{:S(2)}) async-start(bf16[16,2,512]{2,1,0:T(2,128)(2,1)} %reshape.254), calls=%async_computation.4 | async-start | bytes 65536 | tf_op jit(solution)/shard_map/all_to_all | solution.py:124
  62.3 0.1 fusion.32
  62.4 0.1 all_to_all.102
  62.5 0.7 reshape.258
  63.3 5.6 %all-to-all-done.4 = bf16[16,2,512]{2,1,0:T(2,128)(2,1)S(1)} async-done(((bf16[16,2,512]{2,1,0:T(2,128)(2,1)}), bf16[16,2,512]{2,1,0:T(2,128)(2,1)S(1)}, u32[]{:S(2)}, u32[]{:S(2)}) %all-to-all-start.4) | async-done | bytes 32800 | tf_op jit(solution)/shard_map/all_to_all | solution.py:124
  68.9 3.5 %all-to-all-start.2 = ((bf16[16,2,512]{2,1,0:T(2,128)(2,1)}), bf16[16,2,512]{2,1,0:T(2,128)(2,1)S(1)}, u32[]{:S(2)}, u32[]{:S(2)}) async-start(bf16[16,2,512]{2,1,0:T(2,128)(2,1)} %reshape.258), calls=%async_computation.2 | async-start | bytes 65536 | tf_op jit(solution)/shard_map/all_to_all | solution.py:123
  72.4 0.1 reshape.255
  72.5 0.7 gather_fusion.3
  73.3 2.7 %fusion.35 = bf16[128,64]{0,1:T(8,128)(2,1)S(1)} fusion(bf16[128,8192]{1,0:T(8,128)(2,1)} %all-gather.3.cloned.1.call-done, bf16[2,64,8192]{2,1,0:T(8,128)(2,1)} %param.24, bf16[128,64]{0,1:T(8,128)(2,1)S(1)} %copy.87, pred[128]{0:T(512)(128)(4,1)S(1)} %get-tuple-element.6), kind=kOutput, calls=%fused_computation.39 | convolution fusion | flops 134250496 | bytes 3178624 | tf_op jit(solution)/shard_map/dot_general | solution.py:133
  76.0 0.1 copy.88
  76.1 0.7 reshape.256
  76.9 2.1 all-to-all-done.2
  79.0 3.9 %all-to-all-start.5 = ((bf16[16,2,256]{2,1,0:T(2,128)(2,1)}), bf16[16,2,256]{2,1,0:T(2,128)(2,1)S(1)}, u32[]{:S(2)}, u32[]{:S(2)}) async-start(bf16[16,2,256]{2,1,0:T(2,128)(2,1)} %reshape.256), calls=%async_computation.5 | async-start | bytes 32768 | tf_op jit(solution)/shard_map/all_to_all | solution.py:143
  82.8 0.1 reshape.259
  83.0 0.7 gather_fusion.2
  83.8 2.7 %fusion.34 = bf16[128,64]{0,1:T(8,128)(2,1)S(1)} fusion(bf16[128,8192]{1,0:T(8,128)(2,1)} %all-gather.3.cloned.1.call-done, bf16[2,64,8192]{2,1,0:T(8,128)(2,1)} %param.24, bf16[128,64]{0,1:T(8,128)(2,1)S(1)} %copy.82, pred[128]{0:T(512)(128)(4,1)S(1)} %get-tuple-element.6), kind=kOutput, calls=%fused_computation.38 | convolution fusion | flops 134250496 | bytes 3178624 | tf_op jit(solution)/shard_map/dot_general | solution.py:130
  86.5 0.1 copy.83
  86.6 0.7 reshape.260
  87.3 2.0 all-to-all-done.5
  89.3 4.0 %all-to-all-start.3 = ((bf16[16,2,256]{2,1,0:T(2,128)(2,1)}), bf16[16,2,256]{2,1,0:T(2,128)(2,1)S(1)}, u32[]{:S(2)}, u32[]{:S(2)}) async-start(bf16[16,2,256]{2,1,0:T(2,128)(2,1)} %reshape.260), calls=%async_computation.3 | async-start | bytes 32768 | tf_op jit(solution)/shard_map/all_to_all | solution.py:140
  93.3 0.3 fusion
  93.6 0.7 copy.126
  94.3 5.5 %all-to-all-done.3 = bf16[16,2,256]{2,1,0:T(2,128)(2,1)S(1)} async-done(((bf16[16,2,256]{2,1,0:T(2,128)(2,1)}), bf16[16,2,256]{2,1,0:T(2,128)(2,1)S(1)}, u32[]{:S(2)}, u32[]{:S(2)}) %all-to-all-start.3) | async-done | bytes 16416 | tf_op jit(solution)/shard_map/all_to_all | solution.py:140
  99.8 3.5 %all-to-all-start = ((bf16[16,16,512]{2,0,1:T(8,128)(2,1)}), bf16[16,16,512]{2,0,1:T(8,128)(2,1)S(1)}, u32[]{:S(2)}, u32[]{:S(2)}) async-start(bf16[16,16,512]{2,0,1:T(8,128)(2,1)} %bitcast.135), calls=%async_computation | async-start | bytes 524288 | tf_op jit(solution)/shard_map/all_to_all | solution.py:122
  103.4 0.1 reshape.261
  103.7 0.1 reshape.257
  103.8 9.6 %all-to-all-done = bf16[16,16,512]{2,0,1:T(8,128)(2,1)S(1)} async-done(((bf16[16,16,512]{2,0,1:T(8,128)(2,1)}), bf16[16,16,512]{2,0,1:T(8,128)(2,1)S(1)}, u32[]{:S(2)}, u32[]{:S(2)}) %all-to-all-start) | async-done | bytes 262176 | tf_op jit(solution)/shard_map/all_to_all | solution.py:122
  113.4 0.8 gather_fusion
  114.2 5.9 %fusion.28 = bf16[16,8,512]{2,1,0:T(8,128)(2,1)} fusion(bf16[128,8192]{1,0:T(8,128)(2,1)} %all-gather.3.cloned.1.call-done, bf16[8192,512]{1,0:T(8,128)(2,1)} %param.23, bf16[128,512]{1,0:T(8,128)(2,1)S(1)} %gather_fusion, pred[128]{0:T(512)(128)(4,1)S(1)} %get-tuple-element.6), kind=kOutput, calls=%fused_computation.30 | convolution fusion | flops 1074003968 | bytes 10748032 | tf_op jit(solution)/shard_map/dot_general | solution.py:127
  120.2 3.5 %all-to-all-start.1 = ((bf16[16,8,512]{2,1,0:T(8,128)(2,1)}), bf16[16,8,512]{2,1,0:T(8,128)(2,1)S(1)}, u32[]{:S(2)}, u32[]{:S(2)}) async-start(bf16[16,8,512]{2,1,0:T(8,128)(2,1)} %fusion.28), calls=%async_computation.1 | async-start | bytes 262144 | tf_op jit(solution)/shard_map/all_to_all | solution.py:137
  124.0 7.6 %all-to-all-done.1 = bf16[16,8,512]{2,1,0:T(8,128)(2,1)S(1)} async-done(((bf16[16,8,512]{2,1,0:T(8,128)(2,1)}), bf16[16,8,512]{2,1,0:T(8,128)(2,1)S(1)}, u32[]{:S(2)}, u32[]{:S(2)}) %all-to-all-start.1) | async-done | bytes 131104 | tf_op jit(solution)/shard_map/all_to_all | solution.py:137
  131.6 0.2 copy.78
  131.8 0.1 fusion.51
  132.0 0.1 fusion.53
  132.1 0.2 fusion.66
  132.3 0.9 copy-done.1
  133.2 1.0 fusion.84
  134.2 0.3 fusion.54
  134.6 0.6 fusion.29
  135.2 0.8 copy.127
  135.9 39.2 %all-gather.5.cloned.1.call-done = bf16[128,8192]{1,0:T(8,128)(2,1)} async-done(((bf16[8,8192]{1,0:T(8,128)(2,1)}), bf16[128,8192]{1,0:T(8,128)(2,1)}) %all-gather.5.cloned.1.call-update) | async-done | bytes 2097168 | tf_op jit(solution)/shard_map/all_gather | solution.py:150
  175.1 2.7 %fusion.39 = bf16[16,64]{1,0:T(8,128)(2,1)S(1)} fusion(bf16[128,8192]{1,0:T(8,128)(2,1)} %all-gather.5.cloned.1.call-done, bf16[1,4,64,8192]{3,2,1,0:T(8,128)(2,1)} %param.26, s32[128]{0:T(128)S(1)} %broadcast_add_fusion, s32[16]{0:T(128)S(1)} %iota_add_fusion), kind=kOutput, calls=%fused_computation.41 | convolution fusion | flops 50465792 | bytes 3148352 | tf_op jit(solution)/shard_map/dot_general | solution.py:154
  177.8 0.3 fusion.1
  178.1 13.3 %all_to_all.128 = bf16[16,16,512]{2,0,1:T(8,128)(2,1)S(1)} all-to-all(bf16[16,16,512]{2,0,1:T(8,128)(2,1)S(1)} %bitcast.145), channel_id=1, replica_groups=mesh['group'=2,'replica'=16] {'replica'}, dimensions={1} | all-to-all | bytes 524288 | tf_op jit(solution)/shard_map/all_to_all | solution.py:160
  191.5 0.8 gather_fusion.1
  192.2 5.3 %fusion.27 = bf16[16,8,512]{2,1,0:T(8,128)(2,1)S(1)} fusion(bf16[128,8192]{1,0:T(8,128)(2,1)} %all-gather.5.cloned.1.call-done, bf16[8192,512]{1,0:T(8,128)(2,1)} %param.25, f32[128,512]{1,0:T(8,128)S(1)} %gather_fusion.1, pred[128]{0:T(512)(128)(4,1)S(1)} %get-tuple-element.6), kind=kOutput, calls=%fused_computation.29 | convolution fusion | flops 1073938432 | bytes 10879104 | tf_op jit(solution)/shard_map/dot_general | solution.py:163
  197.5 10.7 %all_to_all.129 = bf16[16,8,512]{2,1,0:T(8,128)(2,1)S(1)} all-to-all(bf16[16,8,512]{2,1,0:T(8,128)(2,1)S(1)} %fusion.27), channel_id=1, replica_groups=mesh['group'=2,'replica'=16] {'replica'}, dimensions={0} | all-to-all | bytes 262144 | tf_op jit(solution)/shard_map/all_to_all | solution.py:166
  208.2 0.7 copy.132
  (41 shorter events, 1.0 us)
Async XLA Ops:
  6.5 128.0 %copy-start = (bf16[8,96,1024]{2,1,0:T(8,128)(2,1)S(1)}, bf16[8,96,1024]{2,1,0:T(8,128)(2,1)}, u32[]{:S(2)}) copy-start(bf16[8,96,1024]{2,1,0:T(8,128)(2,1)} %param.22) | copy-start | bytes 4718596
  6.5 47.2 %all-gather.3.cloned.1.call-start = ((), (), s32[]{:S(2)}) async-start(), calls=%async_computation.8 | async-start | bytes 2228224 | tf_op jit(solution)/shard_map/all_gather | solution.py:96
  28.2 29.6 %copy-start.4 = (bf16[1,2,64,1024]{3,2,1,0:T(8,128)(2,1)S(1)}, bf16[1,2,64,1024]{3,2,1,0:T(8,128)(2,1)}, u32[]{:S(2)}) copy-start(bf16[1,2,64,1024]{3,2,1,0:T(8,128)(2,1)} %param.28) | copy-start | bytes 786436
  58.8 10.1 %all-to-all-start.4 = ((bf16[16,2,512]{2,1,0:T(2,128)(2,1)}), bf16[16,2,512]{2,1,0:T(2,128)(2,1)S(1)}, u32[]{:S(2)}, u32[]{:S(2)}) async-start(bf16[16,2,512]{2,1,0:T(2,128)(2,1)} %reshape.254), calls=%async_computation.4 | async-start | bytes 65536 | tf_op jit(solution)/shard_map/all_to_all | solution.py:124
  68.9 10.1 %all-to-all-start.2 = ((bf16[16,2,512]{2,1,0:T(2,128)(2,1)}), bf16[16,2,512]{2,1,0:T(2,128)(2,1)S(1)}, u32[]{:S(2)}, u32[]{:S(2)}) async-start(bf16[16,2,512]{2,1,0:T(2,128)(2,1)} %reshape.258), calls=%async_computation.2 | async-start | bytes 65536 | tf_op jit(solution)/shard_map/all_to_all | solution.py:123
  76.0 17.3 %copy-start.2 = (bf16[1,64,8192]{2,1,0:T(8,128)(2,1)S(1)}, bf16[1,64,8192]{2,1,0:T(8,128)(2,1)}, u32[]{:S(2)}) copy-start(bf16[1,64,8192]{2,1,0:T(8,128)(2,1)} %param.27) | copy-start | bytes 3145732
  79.0 10.4 %all-to-all-start.5 = ((bf16[16,2,256]{2,1,0:T(2,128)(2,1)}), bf16[16,2,256]{2,1,0:T(2,128)(2,1)S(1)}, u32[]{:S(2)}, u32[]{:S(2)}) async-start(bf16[16,2,256]{2,1,0:T(2,128)(2,1)} %reshape.256), calls=%async_computation.5 | async-start | bytes 32768 | tf_op jit(solution)/shard_map/all_to_all | solution.py:143
  89.3 10.5 %all-to-all-start.3 = ((bf16[16,2,256]{2,1,0:T(2,128)(2,1)}), bf16[16,2,256]{2,1,0:T(2,128)(2,1)S(1)}, u32[]{:S(2)}, u32[]{:S(2)}) async-start(bf16[16,2,256]{2,1,0:T(2,128)(2,1)} %reshape.260), calls=%async_computation.3 | async-start | bytes 32768 | tf_op jit(solution)/shard_map/all_to_all | solution.py:140
  99.8 13.5 %all-to-all-start = ((bf16[16,16,512]{2,0,1:T(8,128)(2,1)}), bf16[16,16,512]{2,0,1:T(8,128)(2,1)S(1)}, u32[]{:S(2)}, u32[]{:S(2)}) async-start(bf16[16,16,512]{2,0,1:T(8,128)(2,1)} %bitcast.135), calls=%async_computation | async-start | bytes 524288 | tf_op jit(solution)/shard_map/all_to_all | solution.py:122
  120.2 11.4 %all-to-all-start.1 = ((bf16[16,8,512]{2,1,0:T(8,128)(2,1)}), bf16[16,8,512]{2,1,0:T(8,128)(2,1)S(1)}, u32[]{:S(2)}, u32[]{:S(2)}) async-start(bf16[16,8,512]{2,1,0:T(8,128)(2,1)} %fusion.28), calls=%async_computation.1 | async-start | bytes 262144 | tf_op jit(solution)/shard_map/all_to_all | solution.py:137
  123.7 51.4 %all-gather.5.cloned.1.call-start = ((), (), s32[]{:S(2)}) async-start(), calls=%async_computation.9 | async-start | bytes 2228224 | tf_op jit(solution)/shard_map/all_gather | solution.py:150
  131.8 1.4 copy-start.1
  135.1 42.6 %copy-start.3 = (bf16[1,64,8192]{2,1,0:T(8,128)(2,1)S(1)}, bf16[1,64,8192]{2,1,0:T(8,128)(2,1)}, u32[]{:S(2)}) copy-start(bf16[1,64,8192]{2,1,0:T(8,128)(2,1)} %param.29) | copy-start | bytes 3145732
Sparse Core Ops, SparseCore 0:
  9.6 44.1 all-gather.2
  136.0 39.0 all-gather.4
where the time goes:
time: 216 us
  waiting for transfers between devices  97.2 us (45%)
  blocking collectives  37.8 us (17%)
  matrix products  25.9 us (12%)
  starting transfers between devices  21.9 us (10%)
  between operations  14.4 us (7%)
  local copies, waits for them, and re-layouts  11.9 us (6%)
  other arithmetic  6.6 us (3%)
    all_gather x1, waiting for transfers between devices, local(): lax.all_gather(attention_result, 'replica', axis=0, tiled=True)  39.2 us
    all_gather x1, waiting for transfers between devices, local(): lax.all_gather(normalized_input, 'replica', axis=0, tiled=True)  25.5 us
    unnamed x1, blocking collectives  13.7 us
    all_to_all x1, blocking collectives, local(): lax.all_to_all(output_update.astype(jnp.bfloat16), 'replica', split_axis=...  13.3 us
    all_to_all x1, blocking collectives, local(): lax.all_to_all(partial_cols.astype(jnp.bfloat16), 'replica', split_axis=0...  10.7 us
    all_to_all x1, waiting for transfers between devices, local(): lax.all_to_all(query_update, 'replica', split_axis=1, concat_axis=0, tile...  9.6 us
    all_to_all x1, waiting for transfers between devices, local(): lax.all_to_all(queries.astype(jnp.bfloat16), 'replica', split_axis=0, con...  7.59 us
    unnamed x23, local copies, waits for them, and re-layouts  7.14 us
  transfers between devices with their start and end apart: 8, of which 8 were waited for; matrix products, arithmetic and copies ran while one was open for 7% of the time, Pallas kernels for 0%

commit v1 on v0

--- a/solution.py
+++ b/solution.py
@@ -1,8 +1,11 @@
+import functools
 import math
 
 import jax
 import jax.numpy as jnp
 from jax import lax
+from jax.experimental import pallas as pl
+from jax.experimental.pallas import tpu as pltpu
 from jax.sharding import PartitionSpec as P
 
 HEADS = 64
@@ -168,6 +171,565 @@
     )
 
 
+CHUNKS = 4
+Z_STRIDE = 4
+Z_COUNT = 4
+
+
+def remote(source, target, send_sem, recv_sem, device):
+    return pltpu.make_async_remote_copy(
+        src_ref=source,
+        dst_ref=target,
+        send_sem=send_sem,
+        recv_sem=recv_sem,
+        device_id={"replica": device},
+        device_id_type=pl.DeviceIdType.MESH,
+    )
+
+
+def greet_all(devices, me):
+    barrier = pltpu.get_barrier_semaphore()
+
+    def greet(i, carry):
+        pl.semaphore_signal(
+            barrier,
+            inc=1,
+            device_id={"replica": (me + i) % devices},
+            device_id_type=pl.DeviceIdType.MESH,
+        )
+        return carry
+
+    lax.fori_loop(1, devices, greet, 0)
+    pl.semaphore_wait(barrier, devices - 1)
+
+
+class Gather:
+    def __init__(self, devices, me, blocks, send_sem, recv_sem):
+        self.devices, self.me, self.blocks = devices, me, blocks
+        self.send_sem, self.recv_sem = send_sem, recv_sem
+        self.y_peer = me + 2 - 4 * ((me // 2) % 2)
+        self.core_peer = me + 1 - 2 * (me % 2)
+
+    def copy(self, k, origin, device, number):
+        block = self.blocks.at[k, origin]
+        return remote(
+            block, block, self.send_sem.at[k, number], self.recv_sem.at[k, origin], device
+        )
+
+    def own(self, k):
+        for i in range(1, Z_COUNT):
+            self.copy(k, self.me, (self.me + Z_STRIDE * i) % self.devices, i - 1).start()
+        self.copy(k, self.me, self.y_peer, 3).start()
+        self.copy(k, self.me, self.core_peer, 4).start()
+
+    def pass_z(self, k):
+        for i in range(1, Z_COUNT):
+            origin = (self.me + Z_STRIDE * i) % self.devices
+            self.copy(k, origin, self.y_peer, 0).wait_recv()
+            self.copy(k, origin, self.y_peer, 4 + i).start()
+            self.copy(k, origin, self.core_peer, 7 + i).start()
+
+    def pass_y(self, k):
+        for i in range(Z_COUNT):
+            origin = (self.y_peer + Z_STRIDE * i) % self.devices
+            self.copy(k, origin, self.y_peer, 0).wait_recv()
+            self.copy(k, origin, self.core_peer, 11 + i).start()
+
+    def arrive(self, k):
+        def one(i, carry):
+            origin = (self.core_peer + 2 * i) % self.devices
+            self.copy(k, origin, self.y_peer, 0).wait_recv()
+            return carry
+
+        lax.fori_loop(0, self.devices // 2, one, 0)
+
+    def finish(self):
+        def one(i, carry):
+            for k in range(CHUNKS):
+                self.copy(k, self.me, self.y_peer, i).wait_send()
+            return carry
+
+        lax.fori_loop(0, self.devices - 1, one, 0)
+
+    def run(self, work):
+        self.own(1)
+        self.pass_z(0)
+        for k in range(CHUNKS):
+            if k + 2 < CHUNKS:
+                self.own(k + 2)
+            if k + 1 < CHUNKS:
+                self.pass_z(k + 1)
+            self.pass_y(k)
+            if k > 0:
+                self.arrive(k - 1)
+                work(k - 1)
+        self.arrive(CHUNKS - 1)
+        work(CHUNKS - 1)
+
+
+class Exchange:
+    def __init__(self, devices, me, outgoing, incoming, send_sem, recv_sem):
+        self.devices, self.me, self.outgoing, self.incoming = devices, me, outgoing, incoming
+        self.send_sem, self.recv_sem = send_sem, recv_sem
+
+    def start(self, device):
+        remote(
+            self.outgoing.at[device],
+            self.incoming.at[self.me],
+            self.send_sem.at[device],
+            self.recv_sem.at[self.me],
+            device,
+        ).start()
+
+    def start_all(self):
+        def one(i, carry):
+            self.start((self.me + i) % self.devices)
+            return carry
+
+        lax.fori_loop(1, self.devices, one, 0)
+
+    def arrive(self):
+        self.incoming[self.me] = self.outgoing[self.me]
+
+        def one(i, carry):
+            device = (self.me + i) % self.devices
+            remote(
+                self.outgoing.at[device],
+                self.incoming.at[device],
+                self.send_sem.at[device],
+                self.recv_sem.at[device],
+                device,
+            ).wait_recv()
+            return carry
+
+        lax.fori_loop(1, self.devices, one, 0)
+
+    def finish(self):
+        def one(i, carry):
+            device = (self.me + i) % self.devices
+            remote(
+                self.outgoing.at[device],
+                self.incoming.at[device],
+                self.send_sem.at[device],
+                self.recv_sem.at[device],
+                device,
+            ).wait_send()
+            return carry
+
+        lax.fori_loop(1, self.devices, one, 0)
+
+
+TRANSPOSED = (((1,), (1,)), ((), ()))
+
+
+def project_kernel(
+    devices,
+    hidden_ref,
+    gain_ref,
+    index_ref,
+    table_ref,
+    query_weight_ref,
+    kv_weight_ref,
+    down_ref,
+    query_up_ref,
+    kv_up_ref,
+    q_out,
+    kv_out,
+    place_out,
+    select_out,
+    blocks,
+    owner_blocks,
+    wq,
+    wr,
+    up_q,
+    up_kv,
+    acc_q,
+    acc_r,
+    delta_send,
+    delta_recv,
+    rows_send,
+    rows_recv,
+    gather_send,
+    gather_recv,
+    owner_send,
+    owner_recv,
+    delta_ssem,
+    delta_rsem,
+    rows_ssem,
+    rows_rsem,
+    load_sem,
+):
+    me = lax.axis_index("replica")
+    rows, width = hidden_ref.shape
+    chunk = width // CHUNKS
+    total = devices * rows
+    capacity = 2 * rows
+    columns = wq.shape[1]
+    rank = up_q.shape[0]
+    adapters = table_ref.shape[1]
+    loads = [
+        pltpu.make_async_copy(query_weight_ref, wq, load_sem.at[0]),
+        pltpu.make_async_copy(kv_weight_ref, wr.at[pl.ds(0, 2)], load_sem.at[1]),
+        pltpu.make_async_copy(down_ref.at[0, pl.ds(0, 3)], wr.at[pl.ds(2, 3)], load_sem.at[2]),
+        pltpu.make_async_copy(query_up_ref.at[0], up_q, load_sem.at[3]),
+        pltpu.make_async_copy(kv_up_ref.at[0], up_kv, load_sem.at[4]),
+    ]
+    for load in loads:
+        load.start()
+    values = hidden_ref[...].astype(jnp.float32)
+    scaled = values * lax.rsqrt(jnp.mean(values * values, axis=-1, keepdims=True) + 1e-06)
+    normed = (scaled * gain_ref[...]).astype(jnp.bfloat16)
+    for k in range(CHUNKS):
+        blocks[k, me] = normed[:, k * chunk : (k + 1) * chunk]
+    picked = index_ref[...] == lax.broadcasted_iota(jnp.int32, (rows, adapters), 1)
+    owner = jnp.sum(
+        jnp.where(picked, table_ref[...].astype(jnp.float32), 0.0), axis=1, keepdims=True
+    )
+    owner_blocks[me] = jnp.broadcast_to(owner, (rows, 128)).astype(jnp.bfloat16)
+    greet_all(devices, me)
+
+    def owner_copy(device, origin):
+        return remote(
+            owner_blocks.at[me],
+            owner_blocks.at[origin],
+            owner_send.at[device],
+            owner_recv.at[origin],
+            device,
+        )
+
+    def send_owner(i, carry):
+        owner_copy((me + i) % devices, me).start()
+        return carry
+
+    def wait_owner(i, carry):
+        device = (me + i) % devices
+        owner_copy(device, device).wait_recv()
+        owner_copy(device, device).wait_send()
+        return carry
+
+    gather = Gather(devices, me, blocks, gather_send, gather_recv)
+
+    def work(k):
+        if k == 0:
+            for load in loads:
+                load.wait()
+        x = blocks[k].reshape(total, chunk)
+        part = pl.ds(k * chunk, chunk)
+        q = jnp.dot(x, wq[part, :], preferred_element_type=jnp.float32)
+        r = lax.dot_general(
+            x,
+            wr[:, :, part].reshape(5 * rank, chunk),
+            TRANSPOSED,
+            preferred_element_type=jnp.float32,
+        )
+        if k == 0:
+            acc_q[...] = q
+            acc_r[...] = r
+        else:
+            acc_q[...] += q
+            acc_r[...] += r
+        if k == 0:
+            lax.fori_loop(1, devices, wait_owner, 0)
+            owners = owner_blocks[...].reshape(total, 128).astype(jnp.float32)
+            lane = lax.broadcasted_iota(jnp.int32, (total, 128), 1)
+            member = jnp.where(owners.astype(jnp.int32) == lane, 1.0, 0.0)
+            before = jnp.where(
+                lax.broadcasted_iota(jnp.int32, (total, total), 0)
+                >= lax.broadcasted_iota(jnp.int32, (total, total), 1),
+                1.0,
+                0.0,
+            )
+            running = jnp.dot(
+                before.astype(jnp.bfloat16),
+                member.astype(jnp.bfloat16),
+                preferred_element_type=jnp.float32,
+            )
+            within = jnp.sum(running * member, axis=1, keepdims=True) - 1.0
+            slot = (owners[:, :1] * capacity + within).astype(jnp.int32)
+            slots = lax.broadcasted_iota(jnp.int32, (total, devices * capacity), 1)
+            place_out[...] = jnp.where(slot == slots, 1.0, 0.0).astype(jnp.bfloat16)
+            mine = jnp.where(slot == me * capacity + lane, 1.0, 0.0)
+            select_out[...] = mine.T[:capacity].astype(jnp.bfloat16)
+
+    gather.own(0)
+    lax.fori_loop(1, devices, send_owner, 0)
+    gather.run(work)
+
+    factors = jnp.dot(
+        select_out[...],
+        acc_r[:, 2 * rank :].astype(jnp.bfloat16),
+        preferred_element_type=jnp.float32,
+    ).astype(jnp.bfloat16)
+    kd = (
+        adapter_scale
+        * jnp.dot(factors[:, rank : 2 * rank], up_kv[0], preferred_element_type=jnp.float32)
+    ).astype(jnp.bfloat16)
+    vd = (
+        adapter_scale
+        * jnp.dot(factors[:, 2 * rank :], up_kv[1], preferred_element_type=jnp.float32)
+    ).astype(jnp.bfloat16)
+    for d in range(devices):
+        pair = d // 2
+        delta_send[d, :, columns : columns + 128] = kd[:, pair * 128 : (pair + 1) * 128]
+        delta_send[d, :, columns + 128 :] = vd[:, pair * 128 : (pair + 1) * 128]
+    deltas = Exchange(devices, me, delta_send, delta_recv, delta_ssem, delta_rsem)
+
+    def update(device):
+        begin = pl.multiple_of(device * columns, columns)
+        delta_send[device, :, :columns] = (
+            adapter_scale
+            * jnp.dot(
+                factors[:, :rank],
+                up_q[:, pl.ds(begin, columns)],
+                preferred_element_type=jnp.float32,
+            )
+        ).astype(jnp.bfloat16)
+
+    def update_and_send(i, carry):
+        device = (me + i) % devices
+        update(device)
+        deltas.start(device)
+        return carry
+
+    lax.fori_loop(1, devices, update_and_send, 0)
+    update(me)
+    deltas.arrive()
+    added = jnp.dot(
+        place_out[...],
+        delta_recv[...].reshape(devices * capacity, columns + 256),
+        preferred_element_type=jnp.float32,
+    )
+    rows_send[:, :, :columns] = (
+        (acc_q[...] + added[:, :columns]).astype(jnp.bfloat16).reshape(devices, rows, columns)
+    )
+    even = me % 2 == 0
+    k_added = jnp.where(even, added[:, columns : columns + 64], added[:, columns + 64 : columns + 128])
+    v_added = jnp.where(even, added[:, columns + 128 : columns + 192], added[:, columns + 192 :])
+    rows_send[:, :, columns:] = (
+        (acc_r[:, : 2 * rank] + jnp.concatenate([k_added, v_added], axis=1))
+        .astype(jnp.bfloat16)
+        .reshape(devices, rows, 128)
+    )
+    exchange = Exchange(devices, me, rows_send, rows_recv, rows_ssem, rows_rsem)
+    exchange.start_all()
+    gather.finish()
+    deltas.finish()
+    exchange.arrive()
+    for d in range(devices):
+        q_out[:, d * columns : (d + 1) * columns] = rows_recv[d, :, :columns]
+        kv_out[d] = rows_recv[d, :, columns:]
+    exchange.finish()
+
+
+def output_kernel(
+    devices,
+    attended_ref,
+    place_ref,
+    select_ref,
+    output_weight_ref,
+    down_ref,
+    output_up_ref,
+    out,
+    blocks,
+    wo,
+    wd,
+    up_o,
+    acc_o,
+    acc_f,
+    delta_send,
+    delta_recv,
+    rows_send,
+    rows_recv,
+    gather_send,
+    gather_recv,
+    delta_ssem,
+    delta_rsem,
+    rows_ssem,
+    rows_rsem,
+    load_sem,
+):
+    me = lax.axis_index("replica")
+    rows, width = attended_ref.shape
+    chunk = width // CHUNKS
+    total = devices * rows
+    capacity = 2 * rows
+    columns = wo.shape[1]
+    loads = [
+        pltpu.make_async_copy(output_weight_ref, wo, load_sem.at[0]),
+        pltpu.make_async_copy(down_ref.at[0, 3], wd, load_sem.at[1]),
+        pltpu.make_async_copy(output_up_ref.at[0], up_o, load_sem.at[2]),
+    ]
+    for load in loads:
+        load.start()
+    for k in range(CHUNKS):
+        blocks[k, me] = attended_ref[:, k * chunk : (k + 1) * chunk]
+    greet_all(devices, me)
+    gather = Gather(devices, me, blocks, gather_send, gather_recv)
+
+    def work(k):
+        if k == 0:
+            for load in loads:
+                load.wait()
+        x = blocks[k].reshape(total, chunk)
+        part = pl.ds(k * chunk, chunk)
+        o = jnp.dot(x, wo[part, :], preferred_element_type=jnp.float32)
+        f = lax.dot_general(x, wd[:, part], TRANSPOSED, preferred_element_type=jnp.float32)
+        if k == 0:
+            acc_o[...] = o
+            acc_f[...] = f
+        else:
+            acc_o[...] += o
+            acc_f[...] += f
+
+    gather.own(0)
+    gather.run(work)
+    factors = jnp.dot(
+        select_ref[...], acc_f[...].astype(jnp.bfloat16), preferred_element_type=jnp.float32
+    ).astype(jnp.bfloat16)
+    deltas = Exchange(devices, me, delta_send, delta_recv, delta_ssem, delta_rsem)
+
+    def update(device):
+        begin = pl.multiple_of(device * columns, columns)
+        delta_send[device] = (
+            adapter_scale
+            * jnp.dot(
+                factors, up_o[:, pl.ds(begin, columns)], preferred_element_type=jnp.float32
+            )
+        ).astype(jnp.bfloat16)
+
+    def update_and_send(i, carry):
+        device = (me + i) % devices
+        update(device)
+        deltas.start(device)
+        return carry
+
+    lax.fori_loop(1, devices, update_and_send, 0)
+    update(me)
+    deltas.arrive()
+    added = jnp.dot(
+        place_ref[...],
+        delta_recv[...].reshape(devices * capacity, columns),
+        preferred_element_type=jnp.float32,
+    )
+    rows_send[...] = (acc_o[...] + added).astype(jnp.bfloat16).reshape(devices, rows, columns)
+    exchange = Exchange(devices, me, rows_send, rows_recv, rows_ssem, rows_rsem)
+    exchange.start_all()
+    gather.finish()
+    deltas.finish()
+    exchange.arrive()
+    for d in range(devices):
+        out[:, d * columns : (d + 1) * columns] = rows_recv[d]
+    exchange.finish()
+
+
+def fused(
+    hidden,
+    input_norm_gain,
+    row_adapter_index,
+    adapter_slot_table,
+    cache_length,
+    rotated_key_cache,
+    cached_value_table,
+    query_weight,
+    key_value_weight,
+    output_weight,
+    adapter_down_weight,
+    query_up_weight,
+    key_value_up_weight,
+    output_up_weight,
+):
+    devices = lax.axis_size("replica")
+    rows, width = hidden.shape
+    total, capacity = devices * rows, 2 * rows
+    columns = query_weight.shape[1]
+    rank = query_up_weight.shape[1]
+    bf16, f32 = jnp.bfloat16, jnp.float32
+    in_vmem = pl.BlockSpec(memory_space=pltpu.VMEM)
+    in_any = pl.BlockSpec(memory_space=pl.ANY)
+    dma = pltpu.SemaphoreType.DMA
+    q_rows, kv, place, select = pl.pallas_call(
+        functools.partial(project_kernel, devices),
+        out_shape=(
+            jax.ShapeDtypeStruct((rows, width), bf16),
+            jax.ShapeDtypeStruct((devices, rows, 128), bf16),
+            jax.ShapeDtypeStruct((total, devices * capacity), bf16),
+            jax.ShapeDtypeStruct((capacity, total), bf16),
+        ),
+        in_specs=[in_vmem] * 4 + [in_any] * 5,
+        out_specs=(in_vmem,) * 4,
+        scratch_shapes=[
+            pltpu.VMEM((CHUNKS, devices, rows, width // CHUNKS), bf16),
+            pltpu.VMEM((devices, rows, 128), bf16),
+            pltpu.VMEM((width, columns), bf16),
+            pltpu.VMEM((5, rank, width), bf16),
+            pltpu.VMEM((rank, width), bf16),
+            pltpu.VMEM(key_value_up_weight.shape[1:], bf16),
+            pltpu.VMEM((total, columns), f32),
+            pltpu.VMEM((total, 5 * rank), f32),
+            pltpu.VMEM((devices, capacity, columns + 256), bf16),
+            pltpu.VMEM((devices, capacity, columns + 256), bf16),
+            pltpu.VMEM((devices, rows, columns + 128), bf16),
+            pltpu.VMEM((devices, rows, columns + 128), bf16),
+            dma((CHUNKS, devices)),
+            dma((CHUNKS, devices)),
+            dma((devices,)),
+            dma((devices,)),
+            dma((devices,)),
+            dma((devices,)),
+            dma((devices,)),
+            dma((devices,)),
+            dma((5,)),
+        ],
+        compiler_params=pltpu.CompilerParams(
+            collective_id=0, has_side_effects=True, vmem_limit_bytes=48 * 2**20
+        ),
+        name="project",
+    )(
+        hidden,
+        input_norm_gain.reshape(1, width),
+        row_adapter_index,
+        adapter_slot_table.reshape(1, -1),
+        query_weight,
+        key_value_weight,
+        adapter_down_weight,
+        query_up_weight,
+        key_value_up_weight,
+    )
+    half = kv.shape[-1] // 2
+    k_rows = kv[:, :, :half].transpose(1, 0, 2).reshape(rows, devices * half)
+    v_rows = kv[:, :, half:].transpose(1, 0, 2).reshape(rows, devices * half)
+    attended = attend(q_rows, k_rows, v_rows, cache_length, rotated_key_cache, cached_value_table)
+    return pl.pallas_call(
+        functools.partial(output_kernel, devices),
+        out_shape=jax.ShapeDtypeStruct((rows, width), bf16),
+        in_specs=[in_vmem] * 3 + [in_any] * 3,
+        out_specs=in_vmem,
+        scratch_shapes=[
+            pltpu.VMEM((CHUNKS, devices, rows, width // CHUNKS), bf16),
+            pltpu.VMEM((width, columns), bf16),
+            pltpu.VMEM((rank, width), bf16),
+            pltpu.VMEM((rank, width), bf16),
+            pltpu.VMEM((total, columns), f32),
+            pltpu.VMEM((total, rank), f32),
+            pltpu.VMEM((devices, capacity, columns), bf16),
+            pltpu.VMEM((devices, capacity, columns), bf16),
+            pltpu.VMEM((devices, rows, columns), bf16),
+            pltpu.VMEM((devices, rows, columns), bf16),
+            dma((CHUNKS, devices)),
+            dma((CHUNKS, devices)),
+            dma((devices,)),
+            dma((devices,)),
+            dma((devices,)),
+            dma((devices,)),
+            dma((3,)),
+        ],
+        compiler_params=pltpu.CompilerParams(
+            collective_id=1, has_side_effects=True, vmem_limit_bytes=48 * 2**20
+        ),
+        name="output",
+    )(attended, place, select, output_weight, adapter_down_weight, output_up_weight)
+
+
 def solution(mesh):
     in_specs = (
         P(("group", "replica"), None),
@@ -186,4 +748,5 @@
         P("replica", None, None),
     )
     out_specs = P(("group", "replica"), None)
-    return jax.shard_map(local, mesh=mesh, in_specs=in_specs, out_specs=out_specs, check_vma=False)
+    body = fused if mesh.shape["replica"] == 16 else local
+    return jax.shard_map(body, mesh=mesh, in_specs=in_specs, out_specs=out_specs, check_vma=False)

time: 216 us -> 98 us (0.45)
  waiting for transfers between devices: 97.2 us -> 0 us
  Pallas kernels: 0 us -> 82.5 us
  blocking collectives: 37.8 us -> 0 us
  matrix products: 25.9 us -> 2.69 us
  starting transfers between devices: 21.9 us -> 0 us
  between operations: 14.4 us -> 0.15 us
  other arithmetic: 6.6 us -> 1.15 us
    pallas_call x0 -> x2, Pallas kernels: none -> 82.5 us  [the longest x1 45.4 us: fused(): pl.pallas_call(functools.partial(project_kernel, devices), out_shape=(jax...]
    all_gather x2 -> x0, waiting for transfers between devices: 64.7 us -> none  [the longest x1 39.2 us: local(): lax.all_gather(attention_result, 'replica', axis=0, tiled=True)]
    all_to_all x6 -> x0, waiting for transfers between devices: 32.5 us -> none  [the longest x1 9.6 us: local(): lax.all_to_all(query_update, 'replica', split_axis=1, concat_axis=0, tile...]
    dot_general x10 -> x0, matrix products: 24.2 us -> none  [the longest x1 5.94 us: local(): jnp.dot(all_normed, query_weight, preferred_element_type=jnp.float32)]
    all_to_all x2 -> x0, blocking collectives: 24 us -> none  [the longest x1 13.3 us: local(): lax.all_to_all(output_update.astype(jnp.bfloat16), 'replica', split_axis=...]
    all_to_all x6 -> x0, starting transfers between devices: 21.9 us -> none  [the longest x1 3.98 us: local(): lax.all_to_all(key_new.astype(jnp.bfloat16), 'replica', split_axis=0, con...]
    unnamed x1 -> x0, blocking collectives: 13.7 us -> none
    unnamed x23 -> x27, local copies, waits for them, and re-layouts: 7.14 us -> 10.8 us
  transfers between devices with their start and end apart: 8 -> 0, of which waited for: 8 -> 0; matrix products, arithmetic and copies ran while one was open for 7% -> 0% of each run, Pallas kernels for 0% -> 0%
where the time goes in v1:
time: 98 us; the launch traced here: 97.6 us
  Pallas kernels  82.5 us (84%)
  local copies, waits for them, and re-layouts  11.1 us (11%)
  matrix products  2.69 us (3%)
  other arithmetic  1.15 us (1%)
    pallas_call x1, Pallas kernels, fused(): pl.pallas_call(functools.partial(project_kernel, devices), out_shape=(jax...  45.4 us
    pallas_call x1, Pallas kernels, fused(): pl.pallas_call(functools.partial(output_kernel, devices), out_shape=jax.S...  37.1 us
    unnamed x27, local copies, waits for them, and re-layouts  10.8 us

profile of v1, /device:TPU:0, one launch (start us, length us, event | category | flops | bytes accessed | tf_op | source)
XLA Modules:
  0.0 97.6 jit_solution(18082868604292328963)
XLA Ops:
  0.0 0.0 copy-start
  0.0 0.8 copy.21.index_ref
  0.9 0.0 copy-start.2
  0.9 1.6 %copy-done.2 = bf16[2,64,8192]{2,1,0:T(8,128)(2,1)S(1)} copy-done((bf16[2,64,8192]{2,1,0:T(8,128)(2,1)S(1)}, bf16[2,64,8192]{2,1,0:T(8,128)(2,1)}, u32[]{:S(2)}) %copy-start.2) | copy-done | bytes 2097176
  2.4 0.0 copy-start.4
  2.4 1.2 %copy-done.4 = bf16[1,64,8192]{2,1,0:T(8,128)(2,1)S(1)} copy-done((bf16[1,64,8192]{2,1,0:T(8,128)(2,1)S(1)}, bf16[1,64,8192]{2,1,0:T(8,128)(2,1)}, u32[]{:S(2)}) %copy-start.4) | copy-done | bytes 1048600
  3.7 0.0 copy-start.5
  3.7 0.9 copy-done.5
  4.6 0.0 copy-start.6
  4.6 0.9 copy-done.6
  5.5 0.0 copy-start.7
  5.5 0.8 copy-done.7
  6.3 0.0 copy-start.8
  6.3 0.7 copy-done.8
  6.9 45.4 %project.1 = (bf16[8,8192]{1,0:T(8,128)(2,1)S(1)}, bf16[16,8,128]{2,1,0:T(8,128)(2,1)S(1)}, bf16[128,256]{1,0:T(8,128)(2,1)S(1)}, bf16[16,128]{1,0:T(8,128)(2,1)S(1)}) custom-call(bf16[8,8192]{1,0:T(8,128)(2,1)S(1)} %copy-done.6, f32[1,8192]{1,0:T(1,128)S(1)} %bitcast.58, s32[8,1]{1,0:T(8,128)S(1)} %copy.21.index_ref, s32[1,16]{1,0:T(1,128)S(1)} %bitcast.59, ...), custom_call_target="tpu_custom_call" | custom-call | tf_op jit(solution)/shard_map/project/pallas_call | solution.py:650
  52.3 0.0 copy-start.11
  52.4 0.1 slice_negate_fusion
  52.5 0.0 copy-start.9
  52.5 0.1 copy_bitcast_fusion
  52.6 0.3 copy-done.11
  53.0 0.1 multiply_cosine_fusion
  53.1 0.1 maximum_bitcast_fusion
  53.2 0.1 fusion.22
  53.3 0.0 copy-start.10
  53.3 0.1 convert_bitcast_fusion.1
  53.4 0.1 reshape.157
  53.5 0.1 slice_negate_fusion.1
  53.6 0.1 fusion.33
  53.7 0.2 fusion.30
  53.9 0.1 copy-done.10
  54.0 0.1 iota_compare_fusion
  54.1 0.0 copy-done.9
  54.1 1.9 %fusion.36 = (f32[8,8,8]{2,1,0:T(8,128)S(1)}, f32[8,8,8,96]{3,2,1,0:T(8,128)S(1)}) fusion(bf16[8,8,8,128]{3,2,1,0:T(8,128)(2,1)} %copy-done.10, pred[8,96]{1,0:T(8,128)(4,1)S(1)} %iota_compare_fusion, bf16[8,96,1024]{2,1,0:T(8,128)(2,1)S(1)} %copy-done.9), kind=kOutput, calls=%fused_computation.48 | convolution fusion | flops 12729856 | bytes 1903360 | tf_op jit(solution)/shard_map/rgjd,rtgd->rgjt/dot_general | solution.py:50
  56.0 0.3 fusion.23
  56.3 0.1 reshape.158
  56.4 0.0 copy-done
  56.4 0.0 copy-start.3
  56.4 0.6 fusion.18
  57.0 0.1 copy.62
  57.1 0.5 copy-done.3
  57.6 0.0 copy-start.1
  57.6 2.2 %copy-done.1 = bf16[1,4,64,8192]{3,2,1,0:T(8,128)(2,1)S(1)} copy-done((bf16[1,4,64,8192]{3,2,1,0:T(8,128)(2,1)S(1)}, bf16[1,4,64,8192]{3,2,1,0:T(8,128)(2,1)}, u32[]{:S(2)}) %copy-start.1) | copy-done | bytes 4194328
  59.8 37.1 %output.1 = bf16[8,8192]{1,0:T(8,128)(2,1)S(1)} custom-call(bf16[8,8192]{1,0:T(8,128)(2,1)S(1)} %bitcast.56, bf16[128,256]{1,0:T(8,128)(2,1)S(1)} %get-tuple-element.11.place_ref, bf16[16,128]{1,0:T(8,128)(2,1)S(1)} %get-tuple-element.12.select_ref, bf16[8192,512]{1,0:T(8,128)(2,1)} %output_weight_ref.1, bf16[1,4,64,8192]{3,2,1,0:T(8,128)(2,1)S(1)} %copy-done.1, ...), custom_call_target="tpu_custom_call" | custom-call | tf_op jit(solution)/shard_map/output/pallas_call | solution.py:702
  96.9 0.7 copy.64
  (8 shorter events, 0.1 us)
Async XLA Ops:
  0.0 56.4 %copy-start = (bf16[8,96,1024]{2,1,0:T(8,128)(2,1)S(1)}, bf16[8,96,1024]{2,1,0:T(8,128)(2,1)}, u32[]{:S(2)}) copy-start(bf16[8,96,1024]{2,1,0:T(8,128)(2,1)} %param.20) | copy-start | bytes 4718596
  0.9 1.6 %copy-start.2 = (bf16[2,64,8192]{2,1,0:T(8,128)(2,1)S(1)}, bf16[2,64,8192]{2,1,0:T(8,128)(2,1)}, u32[]{:S(2)}) copy-start(bf16[2,64,8192]{2,1,0:T(8,128)(2,1)} %kv_weight_ref.1) | copy-start | bytes 6291460
  2.4 1.2 %copy-start.4 = (bf16[1,64,8192]{2,1,0:T(8,128)(2,1)S(1)}, bf16[1,64,8192]{2,1,0:T(8,128)(2,1)}, u32[]{:S(2)}) copy-start(bf16[1,64,8192]{2,1,0:T(8,128)(2,1)} %query_up_ref.1) | copy-start | bytes 3145732
  3.7 0.9 copy-start.5
  4.6 0.9 copy-start.6
  5.5 0.8 copy-start.7
  6.3 0.7 copy-start.8
  52.3 0.7 copy-start.11
  52.5 1.6 %copy-start.9 = (bf16[8,96,1024]{2,1,0:T(8,128)(2,1)S(1)}, bf16[8,96,1024]{2,1,0:T(8,128)(2,1)}, u32[]{:S(2)}) copy-start(bf16[8,96,1024]{2,1,0:T(8,128)(2,1)} %param.19) | copy-start | bytes 4718596
  53.3 0.7 copy-start.10
  56.4 1.2 %copy-start.3 = (bf16[1,64,8192]{2,1,0:T(8,128)(2,1)S(1)}, bf16[1,64,8192]{2,1,0:T(8,128)(2,1)}, u32[]{:S(2)}) copy-start(bf16[1,64,8192]{2,1,0:T(8,128)(2,1)} %output_up_ref.1) | copy-start | bytes 3145732
  57.6 2.2 %copy-start.1 = (bf16[1,4,64,8192]{3,2,1,0:T(8,128)(2,1)S(1)}, bf16[1,4,64,8192]{3,2,1,0:T(8,128)(2,1)}, u32[]{:S(2)}) copy-start(bf16[1,4,64,8192]{3,2,1,0:T(8,128)(2,1)} %down_ref.3) | copy-start | bytes 12582916

commit v2 on v1

--- a/solution.py
+++ b/solution.py
@@ -469,9 +469,9 @@
         * jnp.dot(factors[:, 2 * rank :], up_kv[1], preferred_element_type=jnp.float32)
     ).astype(jnp.bfloat16)
     for d in range(devices):
-        pair = d // 2
-        delta_send[d, :, columns : columns + 128] = kd[:, pair * 128 : (pair + 1) * 128]
-        delta_send[d, :, columns + 128 :] = vd[:, pair * 128 : (pair + 1) * 128]
+        delta_send[d, :, columns:] = jnp.concatenate(
+            [kd[:, d * 64 : (d + 1) * 64], vd[:, d * 64 : (d + 1) * 64]], axis=1
+        )
     deltas = Exchange(devices, me, delta_send, delta_recv, delta_ssem, delta_rsem)
 
     def update(device):
@@ -496,17 +496,14 @@
     deltas.arrive()
     added = jnp.dot(
         place_out[...],
-        delta_recv[...].reshape(devices * capacity, columns + 256),
+        delta_recv[...].reshape(devices * capacity, columns + 128),
         preferred_element_type=jnp.float32,
     )
     rows_send[:, :, :columns] = (
         (acc_q[...] + added[:, :columns]).astype(jnp.bfloat16).reshape(devices, rows, columns)
     )
-    even = me % 2 == 0
-    k_added = jnp.where(even, added[:, columns : columns + 64], added[:, columns + 64 : columns + 128])
-    v_added = jnp.where(even, added[:, columns + 128 : columns + 192], added[:, columns + 192 :])
     rows_send[:, :, columns:] = (
-        (acc_r[:, : 2 * rank] + jnp.concatenate([k_added, v_added], axis=1))
+        (acc_r[:, : 2 * rank] + added[:, columns:])
         .astype(jnp.bfloat16)
         .reshape(devices, rows, 128)
     )
@@ -666,8 +663,8 @@
             pltpu.VMEM(key_value_up_weight.shape[1:], bf16),
             pltpu.VMEM((total, columns), f32),
             pltpu.VMEM((total, 5 * rank), f32),
-            pltpu.VMEM((devices, capacity, columns + 256), bf16),
-            pltpu.VMEM((devices, capacity, columns + 256), bf16),
+            pltpu.VMEM((devices, capacity, columns + 128), bf16),
+            pltpu.VMEM((devices, capacity, columns + 128), bf16),
             pltpu.VMEM((devices, rows, columns + 128), bf16),
             pltpu.VMEM((devices, rows, columns + 128), bf16),
             dma((CHUNKS, devices)),
@@ -681,7 +678,7 @@
             dma((5,)),
         ],
         compiler_params=pltpu.CompilerParams(
-            collective_id=0, has_side_effects=True, vmem_limit_bytes=48 * 2**20
+            collective_id=0, has_side_effects=True, vmem_limit_bytes=60 * 2**20
         ),
         name="project",
     )(
@@ -724,7 +721,7 @@
             dma((3,)),
         ],
         compiler_params=pltpu.CompilerParams(
-            collective_id=1, has_side_effects=True, vmem_limit_bytes=48 * 2**20
+            collective_id=1, has_side_effects=True, vmem_limit_bytes=60 * 2**20
         ),
         name="output",
     )(attended, place, select, output_weight, adapter_down_weight, output_up_weight)

time: 98 us -> 93.1 us (0.950)
  local copies, waits for them, and re-layouts: 11.1 us -> 4.13 us
  Pallas kernels: 82.5 us -> 84.1 us
  other arithmetic: 1.15 us -> 2.74 us
    unnamed x27 -> x15, local copies, waits for them, and re-layouts: 10.8 us -> 3.85 us
    pallas_call x1, Pallas kernels: 37.1 us -> 39 us  [fused(): pl.pallas_call(functools.partial(output_kernel, devices), out_shape=jax.S...]
where the time goes in v2:
time: 93.1 us; the launch traced here: 92.9 us
  Pallas kernels  84.1 us (90%)
  local copies, waits for them, and re-layouts  4.13 us (4%)
  other arithmetic  2.74 us (3%)
  matrix products  1.78 us (2%)
    pallas_call x1, Pallas kernels, fused(): pl.pallas_call(functools.partial(project_kernel, devices), out_shape=(jax...  45.1 us
    pallas_call x1, Pallas kernels, fused(): pl.pallas_call(functools.partial(output_kernel, devices), out_shape=jax.S...  39 us
    unnamed x15, local copies, waits for them, and re-layouts  3.85 us

profile of v2, /device:TPU:0, one launch (start us, length us, event | category | flops | bytes accessed | tf_op | source)
XLA Modules:
  0.0 92.9 jit_solution(11334319483590442426)
XLA Ops:
  0.0 0.0 copy-start
  0.0 1.4 %copy.21.index_ref = s32[8,1]{1,0:T(8,128)} copy(s32[8,1]{0,1:T(1,128)} %param.16) | data formatting | bytes 64 | tf_op args[2]
  1.4 45.1 %project.1 = (bf16[8,8192]{1,0:T(8,128)(2,1)}, bf16[16,8,128]{2,1,0:T(8,128)(2,1)}, bf16[128,256]{1,0:T(8,128)(2,1)}, bf16[16,128]{1,0:T(8,128)(2,1)}) custom-call(bf16[8,8192]{1,0:T(8,128)(2,1)} %hidden_ref.1, f32[1,8192]{1,0:T(1,128)} %bitcast.60, s32[8,1]{1,0:T(8,128)} %copy.21.index_ref, s32[1,16]{1,0:T(1,128)} %bitcast.61, ...), custom_call_target="tpu_custom_call" | custom-call | tf_op jit(solution)/shard_map/project/pallas_call | solution.py:647
  46.6 0.0 copy-start.2
  46.6 0.0 copy-start.5
  46.6 1.0 %convert_bitcast_fusion.2 = f32[8,64,128]{2,0,1:T(8,128)S(1)} fusion(bf16[8,8192]{1,0:T(8,128)(2,1)} %get-tuple-element.9), kind=kLoop, calls=%fused_computation.28 | loop fusion | flops 65536 | bytes 393216 | tf_op jit(solution)/shard_map/reshape | solution.py:41
  47.6 0.0 copy-start.4
  47.6 0.1 slice_negate_fusion
  47.7 0.0 copy-start.1
  47.7 0.1 copy_bitcast_fusion
  47.8 0.0 copy-done.2
  47.9 0.0 copy-done.5
  47.9 0.1 multiply_cosine_fusion
  48.0 0.1 maximum_bitcast_fusion
  48.1 0.1 fusion.22
  48.3 0.1 copy-done.4
  48.3 0.7 convert_bitcast_fusion.1
  49.1 0.1 reshape.157
  49.1 0.0 copy-start.3
  49.1 0.1 slice_negate_fusion.1
  49.2 0.1 fusion.33
  49.3 0.2 fusion.30
  49.5 0.1 iota_compare_fusion
  49.6 0.0 copy-done.1
  49.6 1.0 %fusion.36 = (f32[8,8,8]{2,1,0:T(8,128)S(1)}, f32[8,8,8,96]{3,2,1,0:T(8,128)S(1)}) fusion(bf16[8,8,8,128]{3,2,1,0:T(8,128)(2,1)S(1)} %fusion.22, pred[8,96]{1,0:T(8,128)(4,1)S(1)} %iota_compare_fusion, bf16[8,96,1024]{2,1,0:T(8,128)(2,1)S(1)} %copy-done.1), kind=kOutput, calls=%fused_computation.48 | convolution fusion | flops 12729856 | bytes 1903360 | tf_op jit(solution)/shard_map/rgjd,rtgd->rgjt/dot_general | solution.py:50
  50.6 0.3 fusion.23
  50.9 0.0 copy-done.3
  50.9 0.1 reshape.158
  51.0 0.0 copy-done
  51.0 0.6 fusion.18
  51.6 0.8 copy.62
  52.4 39.0 %output.1 = bf16[8,8192]{1,0:T(8,128)(2,1)} custom-call(bf16[8,8192]{1,0:T(8,128)(2,1)} %bitcast.56, bf16[128,256]{1,0:T(8,128)(2,1)} %get-tuple-element.11.place_ref, bf16[16,128]{1,0:T(8,128)(2,1)} %get-tuple-element.12.select_ref, bf16[8192,512]{1,0:T(8,128)(2,1)} %output_weight_ref.1, bf16[1,4,64,8192]{3,2,1,0:T(8,128)(2,1)} %down_ref.3, ...), custom_call_target="tpu_custom_call" | custom-call | tf_op jit(solution)/shard_map/output/pallas_call | solution.py:699
  91.3 1.6 %copy.64 = bf16[8,8192]{1,0:T(8,128)(2,1)} copy(bf16[8,8192]{1,0:T(8,128)(2,1)} %output.1) | data formatting | bytes 262144
  (7 shorter events, 0.1 us)
Async XLA Ops:
  0.0 51.0 %copy-start = (bf16[8,96,1024]{2,1,0:T(8,128)(2,1)S(1)}, bf16[8,96,1024]{2,1,0:T(8,128)(2,1)}, u32[]{:S(2)}) copy-start(bf16[8,96,1024]{2,1,0:T(8,128)(2,1)} %param.20) | copy-start | bytes 4718596
  46.6 1.3 %copy-start.2 = (bf16[8,8192]{1,0:T(8,128)(2,1)S(1)}, bf16[8,8192]{1,0:T(8,128)(2,1)}, u32[]{:S(2)}) copy-start(bf16[8,8192]{1,0:T(8,128)(2,1)} %get-tuple-element.9) | copy-start | bytes 393220
  46.6 1.3 %copy-start.5 = (s32[8]{0:T(128)S(1)}, s32[8]{0:T(128)}, u32[]{:S(2)}) copy-start(s32[8]{0:T(128)} %param.18) | copy-start | bytes 100
  47.6 0.8 copy-start.4
  47.7 1.9 %copy-start.1 = (bf16[8,96,1024]{2,1,0:T(8,128)(2,1)S(1)}, bf16[8,96,1024]{2,1,0:T(8,128)(2,1)}, u32[]{:S(2)}) copy-start(bf16[8,96,1024]{2,1,0:T(8,128)(2,1)} %param.19) | copy-start | bytes 4718596
  49.1 1.8 %copy-start.3 = (f32[8,16,64]{2,0,1:T(8,128)S(1)}, f32[8,16,64]{2,0,1:T(8,128)}, u32[]{:S(2)}) copy-start(f32[8,16,64]{2,0,1:T(8,128)} %get-tuple-element.20) | copy-start | bytes 98308

commit v3 on v2

--- a/solution.py
+++ b/solution.py
@@ -200,7 +200,10 @@
         return carry
 
     lax.fori_loop(1, devices, greet, 0)
-    pl.semaphore_wait(barrier, devices - 1)
+
+
+def await_all(devices):
+    pl.semaphore_wait(pltpu.get_barrier_semaphore(), devices - 1)
 
 
 class Gather:
@@ -334,7 +337,8 @@
     query_up_ref,
     kv_up_ref,
     q_out,
-    kv_out,
+    k_out,
+    v_out,
     place_out,
     select_out,
     blocks,
@@ -366,7 +370,6 @@
     capacity = 2 * rows
     columns = wq.shape[1]
     rank = up_q.shape[0]
-    adapters = table_ref.shape[1]
     loads = [
         pltpu.make_async_copy(query_weight_ref, wq, load_sem.at[0]),
         pltpu.make_async_copy(kv_weight_ref, wr.at[pl.ds(0, 2)], load_sem.at[1]),
@@ -381,12 +384,13 @@
     normed = (scaled * gain_ref[...]).astype(jnp.bfloat16)
     for k in range(CHUNKS):
         blocks[k, me] = normed[:, k * chunk : (k + 1) * chunk]
-    picked = index_ref[...] == lax.broadcasted_iota(jnp.int32, (rows, adapters), 1)
-    owner = jnp.sum(
-        jnp.where(picked, table_ref[...].astype(jnp.float32), 0.0), axis=1, keepdims=True
-    )
-    owner_blocks[me] = jnp.broadcast_to(owner, (rows, 128)).astype(jnp.bfloat16)
+    owner = jnp.zeros((rows, 128), jnp.int32)
+    row = lax.broadcasted_iota(jnp.int32, (rows, 128), 0)
+    for r in range(rows):
+        owner = jnp.where(row == r, table_ref[index_ref[r]], owner)
+    owner_blocks[me] = owner.astype(jnp.float32).astype(jnp.bfloat16)
     greet_all(devices, me)
+    await_all(devices)
 
     def owner_copy(device, origin):
         return remote(
@@ -513,14 +517,73 @@
     deltas.finish()
     exchange.arrive()
     for d in range(devices):
-        q_out[:, d * columns : (d + 1) * columns] = rows_recv[d, :, :columns]
-        kv_out[d] = rows_recv[d, :, columns:]
+        for j in range(columns // HD):
+            q_out[:, d * (columns // HD) + j, :] = rows_recv[d, :, j * HD : (j + 1) * HD].astype(
+                jnp.float32
+            )
+    for g in range(KV_HEADS):
+        first = rows_recv[2 * g, :, columns:].astype(jnp.float32)
+        second = rows_recv[2 * g + 1, :, columns:].astype(jnp.float32)
+        k_out[:, g, :] = jnp.concatenate([first[:, :64], second[:, :64]], axis=1)
+        v_out[:, g, :] = jnp.concatenate([first[:, 64:], second[:, 64:]], axis=1)
     exchange.finish()
+
+
+def attend_row(q, k_new, v_new, cosine, sine, visible, cached_k, cached_v):
+    heads, size = q.shape
+    groups = k_new.shape[0]
+    per_group = heads // groups
+    scale_factor = 1.0 / math.sqrt(size)
+
+    def turn(x):
+        x = x.astype(jnp.float32)
+        turned = x * cosine + pltpu.roll(x, size // 2, 1) * sine
+        return turned.astype(jnp.bfloat16).astype(jnp.float32)
+
+    def spread(x):
+        return jnp.broadcast_to(x[:, None, :], (groups, per_group, size)).reshape(heads, size)
+
+    q_turned = turn(q)
+    wide = (heads, groups * size)
+    mine = (
+        lax.broadcasted_iota(jnp.int32, wide, 0) // per_group
+        == lax.broadcasted_iota(jnp.int32, wide, 1) // size
+    )
+    q_wide = jnp.where(mine, jnp.concatenate([q_turned] * groups, axis=1), 0.0)
+    scores = scale_factor * lax.dot_general(
+        q_wide.astype(jnp.bfloat16), cached_k, TRANSPOSED, preferred_element_type=jnp.float32
+    )
+    own_score = scale_factor * jnp.sum(
+        q_turned * spread(turn(k_new)), axis=1, keepdims=True
+    )
+    masked = jnp.where(visible, scores, -1e30)
+    largest = jnp.maximum(jnp.max(masked, axis=1, keepdims=True), own_score)
+    weights = jnp.where(visible, jnp.exp(masked - largest), 0.0)
+    own_weight = jnp.exp(own_score - largest)
+    denominator = jnp.sum(weights, axis=1, keepdims=True) + own_weight
+    chances = (weights / denominator).astype(jnp.bfloat16)
+    own_chance = (own_weight / denominator).astype(jnp.bfloat16).astype(jnp.float32)
+    mixed = jnp.dot(chances, cached_v, preferred_element_type=jnp.float32)
+    mixed = jnp.concatenate(
+        [
+            mixed[g * per_group : (g + 1) * per_group, g * size : (g + 1) * size]
+            for g in range(groups)
+        ],
+        axis=0,
+    )
+    return mixed + own_chance * spread(v_new.astype(jnp.float32))
 
 
 def output_kernel(
     devices,
-    attended_ref,
+    q_ref,
+    k_ref,
+    v_ref,
+    cosine_ref,
+    sine_ref,
+    length_ref,
+    key_cache_ref,
+    value_cache_ref,
     place_ref,
     select_ref,
     output_weight_ref,
@@ -544,9 +607,20 @@
     rows_ssem,
     rows_rsem,
     load_sem,
+    cached_k,
+    cached_v,
+    attended,
 ):
     me = lax.axis_index("replica")
-    rows, width = attended_ref.shape
+    rows, heads, size = q_ref.shape
+    width = heads * size
+    greet_all(devices, me)
+    cache_loads = [
+        pltpu.make_async_copy(key_cache_ref, cached_k, load_sem.at[3]),
+        pltpu.make_async_copy(value_cache_ref, cached_v, load_sem.at[4]),
+    ]
+    for load in cache_loads:
+        load.start()
     chunk = width // CHUNKS
     total = devices * rows
     capacity = 2 * rows
@@ -558,9 +632,30 @@
     ]
     for load in loads:
         load.start()
-    for k in range(CHUNKS):
-        blocks[k, me] = attended_ref[:, k * chunk : (k + 1) * chunk]
-    greet_all(devices, me)
+    for load in cache_loads:
+        load.wait()
+    length = cached_k.shape[1]
+    for r in range(rows):
+        visible = (
+            lax.broadcasted_iota(jnp.int32, (heads, length), 1) < length_ref[r]
+        )
+        attended[r * heads : (r + 1) * heads, :] = attend_row(
+            q_ref[r],
+            k_ref[r],
+            v_ref[r],
+            cosine_ref[r : r + 1, :],
+            sine_ref[r : r + 1, :],
+            visible,
+            cached_k[r],
+            cached_v[r],
+        )
+    chunk_heads = heads // CHUNKS
+    for h in range(heads):
+        place = h % chunk_heads * size
+        blocks[h // chunk_heads, me, :, place : place + size] = attended[
+            pl.ds(h, rows, stride=heads), :
+        ].astype(jnp.bfloat16)
+    await_all(devices)
     gather = Gather(devices, me, blocks, gather_send, gather_recv)
 
     def work(k):
@@ -642,18 +737,20 @@
     rank = query_up_weight.shape[1]
     bf16, f32 = jnp.bfloat16, jnp.float32
     in_vmem = pl.BlockSpec(memory_space=pltpu.VMEM)
+    in_smem = pl.BlockSpec(memory_space=pltpu.SMEM)
     in_any = pl.BlockSpec(memory_space=pl.ANY)
     dma = pltpu.SemaphoreType.DMA
-    q_rows, kv, place, select = pl.pallas_call(
+    q_rows, k_rows, v_rows, place, select = pl.pallas_call(
         functools.partial(project_kernel, devices),
         out_shape=(
-            jax.ShapeDtypeStruct((rows, width), bf16),
-            jax.ShapeDtypeStruct((devices, rows, 128), bf16),
+            jax.ShapeDtypeStruct((rows, HEADS, HD), f32),
+            jax.ShapeDtypeStruct((rows, KV_HEADS, HD), f32),
+            jax.ShapeDtypeStruct((rows, KV_HEADS, HD), f32),
             jax.ShapeDtypeStruct((total, devices * capacity), bf16),
             jax.ShapeDtypeStruct((capacity, total), bf16),
         ),
-        in_specs=[in_vmem] * 4 + [in_any] * 5,
-        out_specs=(in_vmem,) * 4,
+        in_specs=[in_vmem] * 2 + [in_smem] * 2 + [in_any] * 5,
+        out_specs=(in_vmem,) * 5,
         scratch_shapes=[
             pltpu.VMEM((CHUNKS, devices, rows, width // CHUNKS), bf16),
             pltpu.VMEM((devices, rows, 128), bf16),
@@ -684,22 +781,22 @@
     )(
         hidden,
         input_norm_gain.reshape(1, width),
-        row_adapter_index,
-        adapter_slot_table.reshape(1, -1),
+        row_adapter_index.reshape(rows),
+        adapter_slot_table,
         query_weight,
         key_value_weight,
         adapter_down_weight,
         query_up_weight,
         key_value_up_weight,
     )
-    half = kv.shape[-1] // 2
-    k_rows = kv[:, :, :half].transpose(1, 0, 2).reshape(rows, devices * half)
-    v_rows = kv[:, :, half:].transpose(1, 0, 2).reshape(rows, devices * half)
-    attended = attend(q_rows, k_rows, v_rows, cache_length, rotated_key_cache, cached_value_table)
+    inv_freq = 1000000.0 ** (-(jnp.arange(HD // 2, dtype=f32) * 2.0 / HD))
+    angles = cache_length.astype(f32)[:, None] * inv_freq[None, :]
+    cosine = jnp.concatenate([jnp.cos(angles), jnp.cos(angles)], axis=-1)
+    sine = jnp.concatenate([-jnp.sin(angles), jnp.sin(angles)], axis=-1)
     return pl.pallas_call(
         functools.partial(output_kernel, devices),
         out_shape=jax.ShapeDtypeStruct((rows, width), bf16),
-        in_specs=[in_vmem] * 3 + [in_any] * 3,
+        in_specs=[in_vmem] * 5 + [in_smem] + [in_any] * 2 + [in_vmem] * 2 + [in_any] * 3,
         out_specs=in_vmem,
         scratch_shapes=[
             pltpu.VMEM((CHUNKS, devices, rows, width // CHUNKS), bf16),
@@ -718,13 +815,30 @@
             dma((devices,)),
             dma((devices,)),
             dma((devices,)),
-            dma((3,)),
+            dma((5,)),
+            pltpu.VMEM(rotated_key_cache.shape, bf16),
+            pltpu.VMEM(cached_value_table.shape, bf16),
+            pltpu.VMEM((rows * HEADS, HD), f32),
         ],
         compiler_params=pltpu.CompilerParams(
             collective_id=1, has_side_effects=True, vmem_limit_bytes=60 * 2**20
         ),
         name="output",
-    )(attended, place, select, output_weight, adapter_down_weight, output_up_weight)
+    )(
+        q_rows,
+        k_rows,
+        v_rows,
+        cosine,
+        sine,
+        cache_length,
+        rotated_key_cache,
+        cached_value_table,
+        place,
+        select,
+        output_weight,
+        adapter_down_weight,
+        output_up_weight,
+    )
 
 
 def solution(mesh):

time: 93.1 us -> 91.8 us (0.986)
  Pallas kernels: 84.1 us -> 88.6 us
  local copies, waits for them, and re-layouts: 4.13 us -> 1.57 us
  matrix products: 1.78 us -> 0 us
  other arithmetic: 2.74 us -> 1.46 us
    pallas_call x1, Pallas kernels: 39 us -> 43.2 us  [fused(): pl.pallas_call(functools.partial(output_kernel, devices), out_shape=jax.S...]
    unnamed x15 -> x1, local copies, waits for them, and re-layouts: 3.85 us -> 1.57 us
    dot_general x3 -> x0, matrix products: 1.78 us -> none  [the longest x1 1 us: attend(): jnp.einsum('rgjd,rtgd->rgjt', grouped_q, cached_k, preferred_element_type...]
    reshape x2 -> x0, other arithmetic: 1 us -> none  [attend(): queries.astype(jnp.float32).reshape(row_count, HEADS, HD)]
where the time goes in v3:
time: 91.8 us; the launch traced here: 91.6 us
  Pallas kernels  88.6 us (97%)
  local copies, waits for them, and re-layouts  1.57 us (2%)
  other arithmetic  1.46 us (2%)
    pallas_call x1, Pallas kernels, fused(): pl.pallas_call(functools.partial(project_kernel, devices), out_shape=(jax...  45.4 us
    pallas_call x1, Pallas kernels, fused(): pl.pallas_call(functools.partial(output_kernel, devices), out_shape=jax.S...  43.2 us

profile of v3, /device:TPU:0, one launch (start us, length us, event | category | flops | bytes accessed | tf_op | source)
XLA Modules:
  0.0 91.6 jit_solution(3716975211030332889)
XLA Ops:
  0.0 0.7 convert_element_type.3
  0.7 0.1 fusion
  0.8 0.7 pad_maximum_fusion
  1.5 45.4 %project.1 = (f32[8,64,128]{2,1,0:T(8,128)}, f32[8,8,128]{2,1,0:T(8,128)}, f32[8,8,128]{2,1,0:T(8,128)}, bf16[128,256]{1,0:T(8,128)(2,1)}, bf16[16,128]{1,0:T(8,128)(2,1)}) custom-call(bf16[8,8192]{1,0:T(8,128)(2,1)} %hidden_ref.1, f32[1,8192]{1,0:T(1,128)} %bitcast.2, s32[8]{0:T(128)} %bitcast.3, s32[16]{0:T(128)} %table_ref.1, ...), custom_call_target="tpu_custom_call" | custom-call | tf_op jit(solution)/shard_map/project/pallas_call | solution.py:743
  46.8 43.2 %output.1 = bf16[8,8192]{1,0:T(8,128)(2,1)} custom-call(f32[8,64,128]{2,1,0:T(8,128)} %get-tuple-element.10.q_ref, f32[8,8,128]{2,1,0:T(8,128)} %get-tuple-element.11.k_ref, f32[8,8,128]{2,1,0:T(8,128)} %get-tuple-element.12.v_ref, f32[8,128]{1,0:T(8,128)} %get-tuple-element.18.cosine_ref, f32[8,128]{1,0:T(8,128)} %get-tuple-element.19.sine_ref, ...), custom_call_target="tpu_custom_call" | custom-call | tf_op jit(solution)/shard_map/output/pallas_call | solution.py:796
  90.0 1.6 %copy.16 = bf16[8,8192]{1,0:T(8,128)(2,1)} copy(bf16[8,8192]{1,0:T(8,128)(2,1)} %output.1) | data formatting | bytes 262144
  (1 shorter events, 0.0 us)

commit v4 on v3

--- a/solution.py
+++ b/solution.py
@@ -365,6 +365,7 @@
 ):
     me = lax.axis_index("replica")
     rows, width = hidden_ref.shape
+    greet_all(devices, me)
     chunk = width // CHUNKS
     total = devices * rows
     capacity = 2 * rows
@@ -389,7 +390,6 @@
     for r in range(rows):
         owner = jnp.where(row == r, table_ref[index_ref[r]], owner)
     owner_blocks[me] = owner.astype(jnp.float32).astype(jnp.bfloat16)
-    greet_all(devices, me)
     await_all(devices)
 
     def owner_copy(device, origin):

time: 91.8 us -> 91.6 us (level)
  no operation moved by 1% of the time
where the time goes in v4:
time: 91.6 us; the launch traced here: 91.4 us
  Pallas kernels  88.4 us (97%)
  local copies, waits for them, and re-layouts  1.57 us (2%)
  other arithmetic  1.46 us (2%)
    pallas_call x1, Pallas kernels, fused(): pl.pallas_call(functools.partial(project_kernel, devices), out_shape=(jax...  45.2 us
    pallas_call x1, Pallas kernels, fused(): pl.pallas_call(functools.partial(output_kernel, devices), out_shape=jax.S...  43.2 us

profile of v4, /device:TPU:0, one launch (start us, length us, event | category | flops | bytes accessed | tf_op | source)
XLA Modules:
  0.0 91.4 jit_solution(6348452515101594260)
XLA Ops:
  0.0 0.7 convert_element_type.3
  0.7 0.1 fusion
  0.8 0.7 pad_maximum_fusion
  1.5 45.2 %project.1 = (f32[8,64,128]{2,1,0:T(8,128)}, f32[8,8,128]{2,1,0:T(8,128)}, f32[8,8,128]{2,1,0:T(8,128)}, bf16[128,256]{1,0:T(8,128)(2,1)}, bf16[16,128]{1,0:T(8,128)(2,1)}) custom-call(bf16[8,8192]{1,0:T(8,128)(2,1)} %hidden_ref.1, f32[1,8192]{1,0:T(1,128)} %bitcast.2, s32[8]{0:T(128)} %bitcast.3, s32[16]{0:T(128)} %table_ref.1, ...), custom_call_target="tpu_custom_call" | custom-call | tf_op jit(solution)/shard_map/project/pallas_call | solution.py:743
  46.7 43.2 %output.1 = bf16[8,8192]{1,0:T(8,128)(2,1)} custom-call(f32[8,64,128]{2,1,0:T(8,128)} %get-tuple-element.10.q_ref, f32[8,8,128]{2,1,0:T(8,128)} %get-tuple-element.11.k_ref, f32[8,8,128]{2,1,0:T(8,128)} %get-tuple-element.12.v_ref, f32[8,128]{1,0:T(8,128)} %get-tuple-element.18.cosine_ref, f32[8,128]{1,0:T(8,128)} %get-tuple-element.19.sine_ref, ...), custom_call_target="tpu_custom_call" | custom-call | tf_op jit(solution)/shard_map/output/pallas_call | solution.py:796
  89.9 1.6 %copy.16 = bf16[8,8192]{1,0:T(8,128)(2,1)} copy(bf16[8,8192]{1,0:T(8,128)(2,1)} %output.1) | data formatting | bytes 262144
  (1 shorter events, 0.0 us)
